TPU v7x, 512 devices: a whole 4x8x8 slice. The times are simulated.
512 devices in a mesh: row: 16 (over z, core), col: 16 (over y, x_hi), seed: 2 (over x_lo).
Axes of the slice: x: 4 (x_hi: 2, x_lo: 2; x = x_hi * 2 + x_lo), y: 8, z: 8, core: 2. Of those that a mesh axis runs over, the one named last changes fastest.
Arguments:
- tokens_act: float32 [4096, 768], P(('seed', 'row')), parts along dimension 0, may hold values from -6 to 6
- single_cond: float32 [4096, 384], P(('seed', 'row')), parts along dimension 0, may hold values from -6 to 6
- noise_level: float32 [2], P('seed'), parts along dimension 0, may hold values from 0.04 to 160
- fourier_freq: float32 [256], replicated, may hold values from -4 to 4
- fourier_phase: float32 [256], replicated, may hold values from 0 to 1
- noise_weight: float32 [256, 384], replicated, may hold values from -0.375 to 0.375
- ada_weight: float32 [384, 1536], replicated, may hold values from -0.3125 to 0.3125
- query_gate_weight: float32 [768, 1536], replicated, may hold values from -0.21875 to 0.21875
- kv_weight: float32 [768, 1536], replicated, may hold values from -0.21875 to 0.21875
- out_weight: float32 [768, 768], replicated, may hold values from -0.21875 to 0.21875
- out_gate_weight: float32 [384, 768], replicated, may hold values from -0.3125 to 0.3125
- pair_bias: bfloat16 [16, 2048, 2048], P(None, 'row', 'col'), may hold values from -384 to 384
- relpos_table: float32 [16, 66], replicated, may hold values from -5 to 5
- chain_id: int32 [2048], replicated, may hold values from 0 to 7, never falling along the last dimension, each value on 1 to 1024 neighbouring positions
- residue_index: int32 [2048], replicated, may hold values from 0 to 3071, as said below
Outputs:
- updated: float32 [4096, 768], P(('seed', 'row')), parts along dimension 0
There are 2 independent parts, one for each index of `seed`. A program takes and returns all parts, laid end to end along the dimension named above; an argument that names none is the same for every part. Nothing has to cross between parts.
Inputs may be any that keep to these rules, and one draw needn't show every extreme that they name: `residue_index`: the first token's residue number is 0; residue numbers never fall along the tokens and rise by 1 or 2 from one token to the next. `chain_id`: chain numbers never fall along the tokens.
All inputs are finite; a program needn't handle non-finite values.
Results may differ from a plain program's by a relative error of at most 0.0003.
Values sent between devices are 32-bit elements; how exact they have to be, the bound alone decides.
A program may use at most 64 MiB of HBM per device.

v0:
```python
import math

import jax
import jax.numpy as jnp
from jax import lax
from jax.sharding import PartitionSpec as P

D = 768
HEADS = 16
HEAD_DIM = 48
REL = 32


def spread(value, axis, source):
    kept = jnp.where(lax.axis_index(axis) == source, value, 0).astype(value.dtype)
    return lax.psum(kept, axis)


def joined(part, axis, combine):
    gathered = jax.tree.map(lambda a: lax.all_gather(a, axis), part)

    def take(source):
        return jax.tree.map(lambda a: lax.dynamic_index_in_dim(a, source, 0, False), gathered)

    return lax.fori_loop(
        1, lax.axis_size(axis), lambda source, state: combine(state, take(source)), take(0)
    )


def layer_norm(inputs):
    average = jnp.mean(inputs, axis=-1, keepdims=True)
    centred = inputs - average
    variance = jnp.mean(centred * centred, axis=-1, keepdims=True)
    return centred * lax.rsqrt(variance + 1e-05)


def matmul_high(left, right):
    return jnp.dot(left, right, precision=lax.Precision.HIGHEST, preferred_element_type=jnp.float32)


def relative_bias(relpos_table, chain_query, chain_key, residue_query, residue_key):
    query_count = chain_query.shape[0]
    block_rows = math.gcd(query_count, 64)
    classes = jnp.arange(2 * REL + 2, dtype=jnp.int32)

    def one_block(block_index):
        start = block_index * block_rows
        chain_part = lax.dynamic_slice_in_dim(chain_query, start, block_rows, 0)
        residue_part = lax.dynamic_slice_in_dim(residue_query, start, block_rows, 0)
        offset = jnp.clip(residue_part[:, None] - residue_key[None, :], -REL, REL) + REL
        bucket = jnp.where(chain_part[:, None] == chain_key[None, :], offset, 2 * REL + 1)
        onehot = (bucket[None, :, :] == classes[:, None, None]).astype(jnp.float32)
        return jnp.einsum("hc,cqk->hqk", relpos_table, onehot, precision=lax.Precision.HIGHEST)

    blocks = lax.map(one_block, jnp.arange(query_count // block_rows, dtype=jnp.int32))
    return jnp.transpose(blocks, (1, 0, 2, 3)).reshape(
        relpos_table.shape[0], query_count, chain_key.shape[0]
    )


def widen(totals):
    return jnp.repeat(totals.T, HEAD_DIM, axis=1)


def combine_partial(earlier, later_part):
    top_one, total_one, sum_one = earlier
    top_two, total_two, sum_two = later_part
    row_top = jnp.maximum(top_one, top_two)
    factor_one = jnp.exp(top_one - row_top)
    factor_two = jnp.exp(top_two - row_top)
    return (
        row_top,
        total_one * factor_one + total_two * factor_two,
        sum_one * widen(factor_one) + sum_two * widen(factor_two),
    )


def body(
    tokens_act,
    single_cond,
    noise_level,
    fourier_freq,
    fourier_phase,
    noise_weight,
    ada_weight,
    query_gate_weight,
    kv_weight,
    out_weight,
    out_gate_weight,
    pair_bias,
    relpos_table,
    chain_id,
    residue_index,
):
    row_count = tokens_act.shape[0]
    row_place = lax.axis_index("row")
    col_place = lax.axis_index("col")
    noise_scaled = 0.25 * jnp.log(noise_level[0] / 16.0)
    features = jnp.cos(2.0 * jnp.pi * (noise_scaled * fourier_freq + fourier_phase))
    cond_norm = layer_norm(single_cond + matmul_high(layer_norm(features)[None, :], noise_weight))
    ada_terms = matmul_high(cond_norm, ada_weight)
    modulated = jax.nn.sigmoid(ada_terms[:, :D]) * layer_norm(tokens_act) + ada_terms[:, D:]
    query_gate = matmul_high(modulated, query_gate_weight)
    key_value = spread(matmul_high(modulated, kv_weight), "row", col_place)
    queries = query_gate[:, :D].reshape(row_count, HEADS, HEAD_DIM)
    keys = key_value[:, :D].reshape(row_count, HEADS, HEAD_DIM)
    values = key_value[:, D:].reshape(row_count, HEADS, HEAD_DIM)
    query_start = row_place * row_count
    key_start = col_place * row_count
    relpos = relative_bias(
        relpos_table,
        lax.dynamic_slice_in_dim(chain_id, query_start, row_count, 0),
        lax.dynamic_slice_in_dim(chain_id, key_start, row_count, 0),
        lax.dynamic_slice_in_dim(residue_index, query_start, row_count, 0),
        lax.dynamic_slice_in_dim(residue_index, key_start, row_count, 0),
    )
    score_scale = 1.0 / jnp.sqrt(jnp.float32(HEAD_DIM))
    scores = (
        jnp.einsum("qhd,khd->hqk", queries, keys, precision=lax.Precision.HIGHEST) * score_scale
        + pair_bias.astype(jnp.float32)
        + relpos
    )
    row_top = jnp.max(scores, axis=2)
    weights = jnp.exp(scores - row_top[:, :, None])
    totals = jnp.sum(weights, axis=2)
    partial_value = jnp.einsum(
        "hqk,khd->qhd", weights, values, precision=lax.Precision.HIGHEST
    ).reshape(row_count, D)
    row_top, totals, partial_value = joined(
        (row_top, totals, partial_value), "col", combine_partial
    )
    attended = partial_value / widen(totals)
    gated = jax.nn.sigmoid(query_gate[:, D:]) * attended
    projected = matmul_high(gated, out_weight)
    update = jax.nn.sigmoid(matmul_high(cond_norm, out_gate_weight)) * projected
    return tokens_act + update


def solution(mesh):
    in_specs = (
        P(("seed", "row"), None),
        P(("seed", "row"), None),
        P("seed"),
        P(),
        P(),
        P(),
        P(),
        P(),
        P(),
        P(),
        P(),
        P(None, "row", "col"),
        P(),
        P(),
        P(),
    )
    out_specs = P(("seed", "row"), None)
    return jax.shard_map(body, mesh=mesh, in_specs=in_specs, out_specs=out_specs, check_vma=False)
```

profile of v0, /device:TPU:1, one launch (start us, length us, event | category | flops | bytes accessed | tf_op | source)
XLA Modules:
  0.0 363.8 jit_solution(10303214355945556179)
XLA Ops:
  9.8 1.3 fusion.44
  13.0 1.3 convolution_reduce_fusion
  17.0 2.7 fusion.34
  19.9 3.5 convolution_select_fusion
  24.6 6.2 %while.31 = (s32[]{:T(128)}, f32[2,16,64,128]{3,1,2,0:T(8,128)}, s32[2]{0:T(128)S(1)}, s32[128]{0:T(128)S(1)}, s32[128]{0:T(128)S(1)}, /*index=5*/s32[128]{0:T(1...) while((s32[]{:T(128)}, f32[2,16,64,128]{3,1,2,0:T(8,128)}, ...), condition=%wide.region_8.9_spmd.clone, body=%wide.region_7.8_spmd.clone.sunk | while | flops 104390664 | bytes 596803 | solution.py:55
  26.0 1.7 fusion.71
  29.1 1.7 fusion.71
  31.8 5.0 %fusion.49 = f32[128,1536]{1,0:T(8,128)S(1)} fusion(f32[128,768]{1,0:T(8,128)S(1)} %slice_add_fusion, f32[768,1536]{1,0:T(8,128)} %param.26), kind=kOutput, calls=%fused_computation.76 | convolution fusion | flops 1811939328 | bytes 5898240 | tf_op jit(solution)/shard_map/dot_general | solution.py:38
  38.6 2.6 copy.39
  41.2 104.7 %all-reduce.2.cloned.1.call-done = f32[128,1536]{1,0:T(8,128)} async-done(((f32[128,1536]{1,0:T(8,128)}), f32[128,1536]{1,0:T(8,128)}) %all-reduce.2.cloned.1.call-update) | async-done | bytes 786448 | tf_op jit(solution)/shard_map/psum | solution.py:16
  148.9 3.5 fusion.48
  152.4 1.8 fusion.19
  154.2 1.9 copy.42
  156.2 36.7 %all-gather = f32[256,128]{1,0:T(8,128)} all-gather(f32[16,128]{1,0:T(8,128)S(1)} %get-tuple-element.299), channel_id=2, replica_groups=mesh['row'=16,'col'=16,'seed'=2] {'col'}, dimensions={0}, use_global_device_ids=true | all-gather | bytes 139264 | tf_op jit(solution)/shard_map/all_gather | solution.py:20
  193.7 31.8 %all-gather.1 = f32[256,128]{1,0:T(8,128)} all-gather(f32[16,128]{1,0:T(8,128)S(1)} %fusion.20), channel_id=3, replica_groups=mesh['row'=16,'col'=16,'seed'=2] {'col'}, dimensions={0}, use_global_device_ids=true | all-gather | bytes 139264 | tf_op jit(solution)/shard_map/all_gather | solution.py:20
  226.8 50.2 %all-gather.4.cloned.1.call-done = f32[16,128,768]{2,1,0:T(8,128)} async-done(((f32[1,128,768]{2,1,0:T(8,128)}), f32[16,128,768]{2,1,0:T(8,128)}) %all-gather.4.cloned.1.call-update) | async-done | bytes 6291472 | tf_op jit(solution)/shard_map/all_gather | solution.py:20
  278.2 70.8 %while.30 = (s32[]{:T(128)}, f32[16,128]{1,0:T(8,128)S(1)}, f32[16,128]{1,0:T(8,128)}, f32[128,768]{0,1:T(8,128)S(1)}, f32[16,16,128]{2,1,0:T(8,128)}, /*index=5...) while((s32[]{:T(128)}, f32[16,128]{1,0:T(8,128)S(1)}, ...), condition=%wide.region_12.13_spmd, body=%wide.region_11.12_spmd.sunk | while | flops 309253 | bytes 2875539 | solution.py:25
  278.3 1.3 fusion.67
  279.6 1.3 fusion.68
  283.0 1.3 fusion.67
  284.3 1.3 fusion.68
  287.7 1.3 fusion.67
  289.0 1.3 fusion.68
  292.4 1.3 fusion.67
  293.7 1.3 fusion.68
  297.1 1.3 fusion.67
  298.5 1.3 fusion.68
  301.9 1.3 fusion.67
  303.2 1.3 fusion.68
  306.6 1.3 fusion.67
  307.9 1.3 fusion.68
  311.3 1.3 fusion.67
  312.6 1.3 fusion.68
  316.0 1.3 fusion.67
  317.3 1.3 fusion.68
  320.7 1.3 fusion.67
  322.1 1.3 fusion.68
  325.5 1.3 fusion.67
  326.8 1.3 fusion.68
  330.2 1.3 fusion.67
  331.5 1.3 fusion.68
  334.9 1.3 fusion.67
  336.2 1.3 fusion.68
  339.6 1.3 fusion.67
  340.9 1.3 fusion.68
  345.7 1.3 fusion.68
  351.6 3.6 fusion.26
  355.3 1.7 fusion.18
  (133 shorter events, 52.2 us)
Async XLA Ops:
  6.5 10.5 %copy-start = (f32[384,1536]{1,0:T(8,128)S(1)}, f32[384,1536]{1,0:T(8,128)}, u32[]{:S(2)}) copy-start(f32[384,1536]{1,0:T(8,128)} %param.25) | copy-start | bytes 7077892
  6.5 139.3 %all-reduce.2.cloned.1.call-start = ((), (), s32[]{:S(2)}) async-start(), calls=%async_computation | async-start | bytes 1572864 | tf_op jit(solution)/shard_map/psum | solution.py:16
  8.5 11.2 %copy-start.1 = (f32[128,768]{1,0:T(8,128)S(1)}, f32[128,768]{1,0:T(8,128)}, u32[]{:S(2)}) copy-start(f32[128,768]{1,0:T(8,128)} %param.19) | copy-start | bytes 1179652
  14.3 2.2 copy-start.9
  15.4 1.2 copy-start.11
  16.5 0.5 copy-start.13
  17.0 2.9 copy-start.3
  19.9 4.7 %copy-start.15 = (f32[16,66]{1,0:T(8,128)S(1)}, f32[16,66]{1,0:T(8,128)}, u32[]{:S(2)}) copy-start(f32[16,66]{1,0:T(8,128)} %param.31) | copy-start | bytes 12676
  23.5 7.3 %copy-start.8 = (bf16[16,128,128]{2,1,0:T(8,128)(2,1)S(1)}, bf16[16,128,128]{2,1,0:T(8,128)(2,1)}, u32[]{:S(2)}) copy-start(bf16[16,128,128]{2,1,0:T(8,128)(2,1)} %param.30) | copy-start | bytes 1572868
  23.5 253.6 %all-gather.4.cloned.1.call-start = ((), (), s32[]{:S(2)}) async-start(), calls=%async_computation.1 | async-start | bytes 6684672 | tf_op jit(solution)/shard_map/all_gather | solution.py:20
  36.8 0.9 copy-start.4
  148.9 3.5 copy-start.6
  350.7 4.5 %copy-start.2 = (f32[128,768]{1,0:T(8,128)S(1)}, f32[128,768]{1,0:T(8,128)}, u32[]{:S(2)}) copy-start(f32[128,768]{1,0:T(8,128)} %param.19) | copy-start | bytes 1179652
  350.7 4.5 %copy-start.5 = (f32[128,384]{1,0:T(8,128)S(1)}, f32[128,384]{1,0:T(8,128)}, u32[]{:S(2)}) copy-start(f32[128,384]{1,0:T(8,128)} %param.20) | copy-start | bytes 589828
  350.7 4.5 %copy-start.10 = (f32[384]{0:T(512)S(1)}, f32[384]{0:T(512)}, u32[]{:S(2)}) copy-start(f32[384]{0:T(512)} %copy-done.9) | copy-start | bytes 4612
  350.7 4.6 %copy-start.12 = (f32[128]{0:T(128)S(1)}, f32[128]{0:T(128)}, u32[]{:S(2)}) copy-start(f32[128]{0:T(128)} %copy-done.11) | copy-start | bytes 1540
  350.7 4.6 %copy-start.14 = (f32[128]{0:T(128)S(1)}, f32[128]{0:T(128)}, u32[]{:S(2)}) copy-start(f32[128]{0:T(128)} %copy-done.13) | copy-start | bytes 1540
  351.6 3.6 %copy-start.7 = (f32[384,768]{1,0:T(8,128)S(1)}, f32[384,768]{1,0:T(8,128)}, u32[]{:S(2)}) copy-start(f32[384,768]{1,0:T(8,128)} %param.29) | copy-start | bytes 3538948
Sparse Core Ops, SparseCore 0:
  23.6 122.2 all-reduce.1
  156.3 120.7 all-gather.3
where the time goes:
time: 368 us; the launch traced here: 364 us
  waiting for transfers between devices  155 us (42%)
  blocking collectives  68.5 us (19%)
  other arithmetic  59.6 us (16%)
  local copies, waits for them, and re-layouts  36.6 us (10%)
  matrix products  26.5 us (7%)
  between operations  15.8 us (4%)
    psum x1, waiting for transfers between devices, spread(): return lax.psum(kept, axis)  105 us
    all_gather x2, blocking collectives, joined(): gathered = jax.tree.map(lambda a: lax.all_gather(a, axis), part)  68.5 us
    all_gather x1, waiting for transfers between devices, joined(): gathered = jax.tree.map(lambda a: lax.all_gather(a, axis), part)  50.2 us
    transpose x30, other arithmetic, widen(): return jnp.repeat(totals.T, HEAD_DIM, axis=1)  39.7 us
    dynamic_slice x32, local copies, waits for them, and re-layouts, take(): lax.dynamic_index_in_dim(a, source, 0, False)  19.6 us
    dot_general x6, matrix products, matmul_high(): jnp.dot(left, right, precision=lax.Precision.HIGHEST, preferred_element_t...  17.7 us
    add x15, other arithmetic, combine_partial(): sum_one * widen(factor_one) + sum_two * widen(factor_two)  12.9 us
  transfers between devices with their start and end apart: 2, of which 2 were waited for; matrix products, arithmetic and copies ran while one was open for 5% of the time, Pallas kernels for 0%

commit v1 on v0

v1 whole, which is shorter than its diff:
```python
import jax
import jax.numpy as jnp
from jax import lax
from jax.experimental import pallas as pl
from jax.experimental.pallas import tpu as pltpu
from jax.sharding import PartitionSpec as P

D = 768
HEADS = 16
HEAD_DIM = 48
C_S = 384
REL = 32
TOK = 128
N_ROW = 16
N_COL = 16
SLICES = 8
SLICE_ROWS = TOK // SLICES
MSG_ROWS = 56
MESH = pl.DeviceIdType.MESH
F32 = jnp.float32
BF16 = jnp.bfloat16


def split(value):
    high = value.astype(BF16)
    low = (value - high.astype(F32)).astype(BF16)
    return high, low


def mul(left, right):
    return jnp.dot(left, right, preferred_element_type=F32)


def stacked(value):
    high, low = split(value)
    return jnp.concatenate([high, low], axis=0)


def dot_split(both, right_high, right_low):
    rows = both.shape[0] // 2
    first = mul(both, right_high)
    return first[:rows] + first[rows:] + mul(both[:rows], right_low)


def layer_norm(inputs):
    average = jnp.mean(inputs, axis=-1, keepdims=True)
    centred = inputs - average
    variance = jnp.mean(centred * centred, axis=-1, keepdims=True)
    return centred * lax.rsqrt(variance + 1e-05)


def sigmoid(value):
    return 1.0 / (1.0 + jnp.exp(-value))


def kernel(
    tokens_hbm,
    cond_hbm,
    noise_ref,
    freq_hbm,
    phase_hbm,
    noise_w_hbm,
    ada_w_hbm,
    qg_w_hbm,
    kv_w_hbm,
    out_w_hbm,
    og_w_hbm,
    bias_hbm,
    table_hbm,
    chain_hbm,
    residue_hbm,
    out_ref,
    tokens,
    cond,
    freq,
    phase,
    noise_w,
    ada_w,
    qg_w,
    kv_w,
    out_w,
    og_w,
    bias,
    table,
    chain,
    residue,
    ada,
    modulated,
    block,
    q_high,
    q_low,
    gates,
    out_gate,
    q_t,
    v_t,
    k_high,
    k_low,
    kv_high,
    kv_low,
    scores_bias,
    parts_out,
    parts_in,
    attended,
    load_sems,
    block_send,
    block_recv,
    mate_send,
    mate_recv,
    part_send,
    part_recv,
    att_send,
    att_recv,
):
    row = lax.axis_index("row")
    col = lax.axis_index("col")
    seed = lax.axis_index("seed")
    core = lax.rem(row, 2)
    col_y, col_x = col // 2, lax.rem(col, 2)
    mate = (row + 1 - 2 * core, col, seed)
    is_source = core == col_x

    pairs = (
        (cond_hbm, cond),
        (freq_hbm, freq),
        (phase_hbm, phase),
        (noise_w_hbm, noise_w),
        (ada_w_hbm, ada_w),
        (tokens_hbm, tokens),
        (qg_w_hbm, qg_w),
        (chain_hbm, chain),
        (residue_hbm, residue),
        (table_hbm, table),
        (bias_hbm, bias),
        (og_w_hbm, og_w),
        (kv_w_hbm, kv_w),
        (out_w_hbm, out_w),
    )
    loads = {}
    for number, (source, target) in enumerate(pairs):
        copy = pltpu.make_async_copy(source, target, load_sems.at[number])
        copy.start()
        loads[number] = copy

    barrier = pltpu.get_barrier_semaphore()

    def greet(step, _):
        pl.semaphore_signal(
            barrier,
            inc=1,
            device_id=(row, lax.rem(col + step, N_COL), seed),
            device_id_type=MESH,
        )
        return 0

    def greet_source(step, _):
        source_col = 2 * (2 * step + core) + lax.rem(col, 2)

        @pl.when(jnp.logical_not((row == col) & (source_col == col)))
        def _():
            pl.semaphore_signal(
                barrier, inc=1, device_id=(col, source_col, seed), device_id_type=MESH
            )

        return 0

    lax.fori_loop(0, SLICES // 2, greet_source, 0)
    lax.fori_loop(1, N_COL, greet, 0)
    pl.semaphore_signal(barrier, inc=1, device_id=mate, device_id_type=MESH)
    to_self = (row == col) & (lax.rem(col_y, 2) == core)
    expected = (
        N_COL - 1 + 1 + jnp.where(is_source, SLICES, 0) - jnp.where(to_self, 1, 0)
    )

    for number in (0, 1, 2, 3):
        loads[number].wait()
    level = jnp.full((2, 128), noise_ref[0, 0], F32)
    noise_scaled = 0.25 * jnp.log(level / 16.0)
    features = jnp.cos(2.0 * jnp.pi * (noise_scaled * freq[...] + phase[...]))
    average = jnp.sum(features, keepdims=True) / 256.0
    centred = features - average
    variance = jnp.sum(centred * centred, keepdims=True) / 256.0
    features = centred * lax.rsqrt(variance + 1e-05)
    feature_row = jnp.concatenate([features[0:1], features[1:2]], axis=1)
    feature_rows = jnp.broadcast_to(feature_row, (16, 256))
    noise_high, noise_low = split(noise_w[...])
    shift = dot_split(stacked(feature_rows), noise_high, noise_low)[0:1]
    cond_both = stacked(layer_norm(cond[...] + shift))

    loads[4].wait()

    def ada_step(step, _):
        columns = pl.ds(pl.multiple_of(step * 256, 256), 256)
        high, low = split(ada_w[:, columns])
        ada[:, columns] = dot_split(cond_both, high, low)
        return 0

    lax.fori_loop(0, 2 * D // 256, ada_step, 0)
    loads[5].wait()
    modulated[...] = (
        sigmoid(ada[:, :D]) * layer_norm(tokens[...]) + ada[:, D:]
    ).reshape(SLICES, SLICE_ROWS, D)

    pl.semaphore_wait(barrier, expected)

    def block_copy(step, piece):
        target_row = 2 * lax.rem(row // 2 + step, 8) + lax.rem(col_y, 2)
        return pltpu.make_async_remote_copy(
            src_ref=modulated.at[piece],
            dst_ref=block.at[piece],
            send_sem=block_send.at[step],
            recv_sem=block_recv.at[piece],
            device_id=(target_row, row, seed),
            device_id_type=MESH,
        )

    @pl.when(is_source)
    def _():
        def send(step, _):
            place = 7 - step

            @pl.when(jnp.logical_not((place == 0) & to_self))
            def _():
                block_copy(place, col_y).start()

            return 0

        lax.fori_loop(0, 8, send, 0)

    @pl.when(is_source & to_self)
    def _():
        block[pl.ds(col_y, 1)] = modulated[pl.ds(col_y, 1)]

    mod_both = stacked(modulated[...].reshape(TOK, D))
    loads[6].wait()

    def query_step(step, _):
        columns = pl.ds(pl.multiple_of(step * 256, 256), 256)
        high, low = split(qg_w[:, columns])
        result = dot_split(mod_both, high, low) * (HEAD_DIM**-0.5)
        q_t[columns, :] = result.T
        return 0

    lax.fori_loop(0, D // 256, query_step, 0)

    def gate_step(step, _):
        columns = pl.ds(pl.multiple_of(step * 256, 256), 256)
        high, low = split(qg_w[:, pl.ds(pl.multiple_of(D + step * 256, 256), 256)])
        gates[:, columns] = sigmoid(dot_split(mod_both, high, low))
        return 0

    lax.fori_loop(0, D // 256, gate_step, 0)
    window_row = lax.broadcasted_iota(jnp.int32, (256, TOK), 0)

    def window_of(head):
        return jnp.minimum(head * HEAD_DIM // 128, D // 128 - 2)

    def query_mask(head, _):
        start = pl.multiple_of(window_of(head) * 128, 128)
        place = head * HEAD_DIM - start
        inside = (window_row >= place) & (window_row < place + HEAD_DIM)
        high, low = split(jnp.where(inside, q_t[pl.ds(start, 256), :], 0.0))
        q_high[head] = high
        q_low[head] = low
        return 0

    lax.fori_loop(0, HEADS, query_mask, 0)

    for number in (7, 8, 9, 10):
        loads[number].wait()
    chain_f = chain[...].astype(F32)
    residue_f = residue[...].astype(F32)
    place = lax.broadcasted_iota(jnp.int32, (N_ROW, TOK), 0)

    def pick(values, which):
        chosen = jnp.sum(jnp.where(place == which, values, 0.0), axis=0, keepdims=True)
        return jnp.broadcast_to(chosen, (TOK, TOK))

    same = pick(chain_f, row) == pick(chain_f, col).T
    offset = jnp.clip(pick(residue_f, row) - pick(residue_f, col).T, -REL, REL) + REL
    bucket = jnp.where(same, offset, 2.0 * REL + 1.0).astype(jnp.int32)
    wide = jnp.concatenate(
        [table[...], jnp.zeros((HEADS, 128 - 2 * REL - 2), F32)], axis=1
    )
    table_rows = [wide[head : head + 1] for head in range(HEADS)]
    for head in range(HEADS):
        rel = jnp.take_along_axis(
            jnp.broadcast_to(table_rows[head], (TOK, 128)), bucket, axis=1
        )
        scores_bias[head] = bias[head].astype(F32).T + rel

    loads[11].wait()

    def out_gate_step(step, _):
        columns = pl.ds(pl.multiple_of(step * 256, 256), 256)
        high, low = split(og_w[:, columns])
        out_gate[:, columns] = sigmoid(dot_split(cond_both, high, low))
        return 0

    lax.fori_loop(0, D // 256, out_gate_step, 0)
    loads[12].wait()

    def kv_split(step, _):
        columns = pl.ds(pl.multiple_of(step * 256, 256), 256)
        high, low = split(kv_w[:, columns])
        kv_high[:, columns] = high
        kv_low[:, columns] = low
        return 0

    lax.fori_loop(0, 2 * D // 256, kv_split, 0)

    def mate_copy(piece):
        return pltpu.make_async_remote_copy(
            src_ref=block.at[piece],
            dst_ref=block.at[piece],
            send_sem=mate_send.at[piece],
            recv_sem=mate_recv.at[piece],
            device_id=mate,
            device_id_type=MESH,
        )

    def pass_on(step, _):
        piece = 2 * step + core

        @pl.when(jnp.logical_not(to_self & (piece == col_y)))
        def _():
            block_copy(0, piece).wait_recv()

        mate_copy(piece).start()
        return 0

    lax.fori_loop(0, SLICES // 2, pass_on, 0)

    def from_mate(step, _):
        mate_copy(2 * step + 1 - core).wait_recv()
        return 0

    lax.fori_loop(0, SLICES // 2, from_mate, 0)

    block_both = stacked(block[...].reshape(TOK, D))

    def key_step(step, _):
        columns = pl.ds(pl.multiple_of(step * 256, 256), 256)
        high, low = split(dot_split(block_both, kv_high[:, columns], kv_low[:, columns]))
        k_high[:, columns] = high
        k_low[:, columns] = low
        return 0

    lax.fori_loop(0, D // 256, key_step, 0)

    def value_step(step, _):
        columns = pl.ds(pl.multiple_of(step * 256, 256), 256)
        source = pl.ds(pl.multiple_of(D + step * 256, 256), 256)
        v_t[columns, :] = dot_split(block_both, kv_high[:, source], kv_low[:, source]).T
        return 0

    lax.fori_loop(0, D // 256, value_step, 0)

    ones_rows = jnp.where(lax.broadcasted_iota(jnp.int32, (16, TOK), 0) == 0, 1.0, 0.0)
    tail_row = lax.broadcasted_iota(jnp.int32, (8, TOK), 0)

    def one_head(head):
        keys = pl.ds(pl.multiple_of(window_of(head) * 128, 128), 256)
        keys_high, keys_low = k_high[:, keys], k_low[:, keys]
        queries = q_high[head]
        scores = (
            mul(keys_high, queries)
            + mul(keys_low, queries)
            + mul(keys_high, q_low[head])
            + scores_bias[head]
        )
        top = jnp.max(scores, axis=0, keepdims=True)
        weights_high, weights_low = split(jnp.exp(scores - top))
        values = v_t[pl.ds(pl.multiple_of(head * HEAD_DIM, 16), HEAD_DIM), :]
        values_high, values_low = split(jnp.concatenate([values, ones_rows], axis=0))
        sums = (
            mul(values_high, weights_high)
            + mul(values_low, weights_high)
            + mul(values_high, weights_low)
        )
        tail = jnp.where(tail_row == 1, top, sums[HEAD_DIM:MSG_ROWS])
        return sums[:HEAD_DIM], tail

    def part_copy(head):
        return pltpu.make_async_remote_copy(
            src_ref=parts_out.at[head],
            dst_ref=parts_in.at[col],
            send_sem=part_send.at[head],
            recv_sem=part_recv.at[col],
            device_id=(row, head, seed),
            device_id_type=MESH,
        )

    def head_group(group, _):
        for member in range(3):
            head = lax.rem(col + 1 + group * 3 + member, HEADS)
            sums, tail = one_head(head)
            parts_out[head, :HEAD_DIM] = sums
            parts_out[head, HEAD_DIM:] = tail
            part_copy(head).start()
        return 0

    lax.fori_loop(0, 5, head_group, 0)
    sums, tail = one_head(col)
    parts_in[col, :HEAD_DIM] = sums
    parts_in[col, HEAD_DIM:] = tail

    def part_arrived(step, _):
        other = lax.rem(col + N_COL - step, N_COL)
        pltpu.make_async_remote_copy(
            src_ref=parts_out.at[other],
            dst_ref=parts_in.at[other],
            send_sem=part_send.at[other],
            recv_sem=part_recv.at[other],
            device_id=(row, other, seed),
            device_id_type=MESH,
        ).wait_recv()
        return 0

    lax.fori_loop(1, N_COL, part_arrived, 0)
    tops = parts_in[:, HEAD_DIM + 1 : HEAD_DIM + 2, :]
    factors = jnp.exp(tops - jnp.max(tops, axis=0, keepdims=True))
    total = jnp.sum(factors * parts_in[:, HEAD_DIM : HEAD_DIM + 1, :], axis=0)
    weighted = jnp.sum(factors * parts_in[:, :HEAD_DIM, :], axis=0)
    attended[pl.ds(col, 1)] = (weighted / total)[None]

    def att_copy(other, place):
        return pltpu.make_async_remote_copy(
            src_ref=attended.at[place],
            dst_ref=attended.at[place],
            send_sem=att_send.at[other],
            recv_sem=att_recv.at[place],
            device_id=(row, other, seed),
            device_id_type=MESH,
        )

    def att_start(step, _):
        att_copy(lax.rem(col + step, N_COL), col).start()
        return 0

    lax.fori_loop(1, N_COL, att_start, 0)
    loads[13].wait()

    def att_arrived(step, _):
        other = lax.rem(col + N_COL - step, N_COL)
        att_copy(other, other).wait_recv()
        return 0

    lax.fori_loop(1, N_COL, att_arrived, 0)
    gated_both = stacked(gates[...] * attended[...].reshape(D, TOK).T)

    def out_step(step, _):
        columns = pl.ds(pl.multiple_of(step * 256, 256), 256)
        high, low = split(out_w[:, columns])
        out_ref[:, columns] = tokens[:, columns] + out_gate[:, columns] * dot_split(
            gated_both, high, low
        )
        return 0

    lax.fori_loop(0, D // 256, out_step, 0)

    @pl.when(is_source)
    def _():
        def sent(step, _):
            @pl.when(jnp.logical_not((step == 0) & to_self))
            def _():
                block_copy(step, col_y).wait_send()

            return 0

        lax.fori_loop(0, 8, sent, 0)

    def mate_sent(step, _):
        mate_copy(2 * step + core).wait_send()
        return 0

    lax.fori_loop(0, SLICES // 2, mate_sent, 0)

    def parts_sent(step, _):
        other = lax.rem(col + step, N_COL)
        part_copy(other).wait_send()
        att_copy(other, col).wait_send()
        return 0

    lax.fori_loop(1, N_COL, parts_sent, 0)


def body(
    tokens_act,
    single_cond,
    noise_level,
    fourier_freq,
    fourier_phase,
    noise_weight,
    ada_weight,
    query_gate_weight,
    kv_weight,
    out_weight,
    out_gate_weight,
    pair_bias,
    relpos_table,
    chain_id,
    residue_index,
):
    hbm = pl.BlockSpec(memory_space=pl.ANY)
    vmem = pltpu.VMEM
    dma = pltpu.SemaphoreType.DMA
    return pl.pallas_call(
        kernel,
        name="attention_block",
        out_shape=jax.ShapeDtypeStruct((TOK, D), F32),
        in_specs=[hbm, hbm, pl.BlockSpec(memory_space=pltpu.SMEM)] + [hbm] * 12,
        out_specs=pl.BlockSpec(memory_space=pltpu.VMEM),
        scratch_shapes=[
            vmem((TOK, D), F32),
            vmem((TOK, C_S), F32),
            vmem((2, 128), F32),
            vmem((2, 128), F32),
            vmem((256, C_S), F32),
            vmem((C_S, 2 * D), F32),
            vmem((D, 2 * D), F32),
            vmem((D, 2 * D), F32),
            vmem((D, D), F32),
            vmem((C_S, D), F32),
            vmem((HEADS, TOK, TOK), BF16),
            vmem((HEADS, 2 * REL + 2), F32),
            vmem((N_ROW, TOK), jnp.int32),
            vmem((N_ROW, TOK), jnp.int32),
            vmem((TOK, 2 * D), F32),
            vmem((SLICES, SLICE_ROWS, D), F32),
            vmem((SLICES, SLICE_ROWS, D), F32),
            vmem((HEADS, 256, TOK), BF16),
            vmem((HEADS, 256, TOK), BF16),
            vmem((TOK, D), F32),
            vmem((TOK, D), F32),
            vmem((D, TOK), F32),
            vmem((D, TOK), F32),
            vmem((TOK, D), BF16),
            vmem((TOK, D), BF16),
            vmem((D, 2 * D), BF16),
            vmem((D, 2 * D), BF16),
            vmem((HEADS, TOK, TOK), F32),
            vmem((HEADS, MSG_ROWS, TOK), F32),
            vmem((N_COL, MSG_ROWS, TOK), F32),
            vmem((HEADS, HEAD_DIM, TOK), F32),
            dma((14,)),
            dma((8,)),
            dma((SLICES,)),
            dma((SLICES,)),
            dma((SLICES,)),
            dma((N_COL,)),
            dma((N_COL,)),
            dma((N_COL,)),
            dma((N_COL,)),
        ],
        compiler_params=pltpu.CompilerParams(
            collective_id=0, has_side_effects=True, vmem_limit_bytes=48 * 1024 * 1024
        ),
    )(
        tokens_act,
        single_cond,
        noise_level.reshape(1, 1),
        fourier_freq.reshape(2, 128),
        fourier_phase.reshape(2, 128),
        noise_weight,
        ada_weight,
        query_gate_weight,
        kv_weight,
        out_weight,
        out_gate_weight,
        pair_bias,
        relpos_table,
        chain_id.reshape(N_ROW, TOK),
        residue_index.reshape(N_ROW, TOK),
    )


def solution(mesh):
    in_specs = (
        P(("seed", "row"), None),
        P(("seed", "row"), None),
        P("seed"),
        P(),
        P(),
        P(),
        P(),
        P(),
        P(),
        P(),
        P(),
        P(None, "row", "col"),
        P(),
        P(),
        P(),
    )
    out_specs = P(("seed", "row"), None)
    return jax.shard_map(body, mesh=mesh, in_specs=in_specs, out_specs=out_specs, check_vma=False)
```

time: 368 us -> 86.8 us (0.24)
  waiting for transfers between devices: 155 us -> 0 us
  Pallas kernels: 0 us -> 73.9 us
  blocking collectives: 68.5 us -> 0 us
  other arithmetic: 59.6 us -> 0 us
  matrix products: 26.5 us -> 0 us
  local copies, waits for them, and re-layouts: 36.6 us -> 11.1 us
  between operations: 15.8 us -> 0.68 us
    psum x1 -> x0, waiting for transfers between devices: 105 us -> none  [spread(): return lax.psum(kept, axis)]
    pallas_call x0 -> x1, Pallas kernels: none -> 73.9 us  [body(): pl.pallas_call(kernel, name='attention_block', out_shape=jax.ShapeDtypeSt...]
    all_gather x2 -> x0, blocking collectives: 68.5 us -> none  [joined(): gathered = jax.tree.map(lambda a: lax.all_gather(a, axis), part)]
    all_gather x1 -> x0, waiting for transfers between devices: 50.2 us -> none  [joined(): gathered = jax.tree.map(lambda a: lax.all_gather(a, axis), part)]
    transpose x30 -> x0, other arithmetic: 39.7 us -> none  [widen(): return jnp.repeat(totals.T, HEAD_DIM, axis=1)]
    dot_general x10 -> x0, matrix products: 26.5 us -> none  [the longest x6 17.7 us: matmul_high(): jnp.dot(left, right, precision=lax.Precision.HIGHEST, preferred_element_t...]
    dynamic_slice x39 -> x0, local copies, waits for them, and re-layouts: 22 us -> none  [the longest x32 19.6 us: take(): lax.dynamic_index_in_dim(a, source, 0, False)]
    add x16 -> x0, other arithmetic: 13.1 us -> none  [the longest x15 12.9 us: combine_partial(): sum_one * widen(factor_one) + sum_two * widen(factor_two)]
  transfers between devices with their start and end apart: 2 -> 0, of which waited for: 2 -> 0; matrix products, arithmetic and copies ran while one was open for 5% -> 0% of each run, Pallas kernels for 0% -> 0%
where the time goes in v1:
time: 86.8 us; the launch traced here: 85.7 us
  Pallas kernels  73.9 us (85%)
  local copies, waits for them, and re-layouts  11.1 us (13%)
    pallas_call x1, Pallas kernels, body(): pl.pallas_call(kernel, name='attention_block', out_shape=jax.ShapeDtypeSt...  73.9 us
    unnamed x23, local copies, waits for them, and re-layouts  11.1 us

profile of v1, /device:TPU:1, one launch (start us, length us, event | category | flops | bytes accessed | tf_op | source)
XLA Modules:
  0.0 85.7 jit_solution(15028556141417318023)
XLA Ops:
  0.7 0.0 copy-start
  0.7 1.7 %copy-done = f32[384,1536]{1,0:T(8,128)S(1)} copy-done((f32[384,1536]{1,0:T(8,128)S(1)}, f32[384,1536]{1,0:T(8,128)}, u32[]{:S(2)}) %copy-start) | copy-done | bytes 2359320
  2.3 0.0 copy-start.1
  2.3 1.3 %copy-done.1 = f32[384,768]{1,0:T(8,128)S(1)} copy-done((f32[384,768]{1,0:T(8,128)S(1)}, f32[384,768]{1,0:T(8,128)}, u32[]{:S(2)}) %copy-start.1) | copy-done | bytes 1179672
  3.6 0.0 copy-start.2
  3.6 1.0 %copy-done.2 = bf16[16,128,128]{2,1,0:T(8,128)(2,1)S(1)} copy-done((bf16[16,128,128]{2,1,0:T(8,128)(2,1)S(1)}, bf16[16,128,128]{2,1,0:T(8,128)(2,1)}, u32[]{:S(2)}) %copy-start.2) | copy-done | bytes 524312
  4.6 0.0 copy-start.3
  4.6 1.0 %copy-done.3 = f32[128,768]{1,0:T(8,128)S(1)} copy-done((f32[128,768]{1,0:T(8,128)S(1)}, f32[128,768]{1,0:T(8,128)}, u32[]{:S(2)}) %copy-start.3) | copy-done | bytes 393240
  5.6 0.0 copy-start.4
  5.6 1.0 %copy-done.4 = f32[256,384]{1,0:T(8,128)S(1)} copy-done((f32[256,384]{1,0:T(8,128)S(1)}, f32[256,384]{1,0:T(8,128)}, u32[]{:S(2)}) %copy-start.4) | copy-done | bytes 393240
  6.6 0.0 copy-start.5
  6.6 0.9 %copy-done.5 = f32[128,384]{1,0:T(8,128)S(1)} copy-done((f32[128,384]{1,0:T(8,128)S(1)}, f32[128,384]{1,0:T(8,128)}, u32[]{:S(2)}) %copy-start.5) | copy-done | bytes 196632
  7.6 0.0 copy-start.6
  7.6 0.7 copy-done.6
  8.2 0.0 copy-start.7
  8.3 0.7 copy-done.7
  8.9 0.0 copy-start.8
  8.9 0.7 copy-done.8
  9.6 0.0 copy-start.9
  9.6 0.7 copy-done.9
  10.3 0.0 copy-start.10
  10.3 0.7 copy-done.10
  11.0 73.9 %attention_block.1 = f32[128,768]{1,0:T(8,128)S(1)} custom-call(f32[128,768]{1,0:T(8,128)S(1)} %copy-done.3, f32[128,384]{1,0:T(8,128)S(1)} %copy-done.5, f32[1,1]{1,0:T(1,128)} %bitcast.5.noise_ref, f32[2,128]{1,0:T(2,128)S(1)} %bitcast.8, f32[2,128]{1,0:T(2,128)S(1)} %bitcast.9, f32[256,384]{1,0:T(8,128)S(1)} %copy-done.4, f32[384,1536]{1,0:T(8,128)S(1)} %copy-done, ...), custom_call_target="tpu_custom_call" | custom-call | tf_op jit(solution)/shard_map/attention_block/pallas_call | solution.py:507
  85.0 0.7 copy.18
Async XLA Ops:
  0.7 1.7 %copy-start = (f32[384,1536]{1,0:T(8,128)S(1)}, f32[384,1536]{1,0:T(8,128)}, u32[]{:S(2)}) copy-start(f32[384,1536]{1,0:T(8,128)} %ada_w_hbm.1) | copy-start | bytes 7077892
  2.3 1.3 %copy-start.1 = (f32[384,768]{1,0:T(8,128)S(1)}, f32[384,768]{1,0:T(8,128)}, u32[]{:S(2)}) copy-start(f32[384,768]{1,0:T(8,128)} %og_w_hbm.1) | copy-start | bytes 3538948
  3.6 1.0 %copy-start.2 = (bf16[16,128,128]{2,1,0:T(8,128)(2,1)S(1)}, bf16[16,128,128]{2,1,0:T(8,128)(2,1)}, u32[]{:S(2)}) copy-start(bf16[16,128,128]{2,1,0:T(8,128)(2,1)} %bias_hbm.1) | copy-start | bytes 1572868
  4.6 1.0 %copy-start.3 = (f32[128,768]{1,0:T(8,128)S(1)}, f32[128,768]{1,0:T(8,128)}, u32[]{:S(2)}) copy-start(f32[128,768]{1,0:T(8,128)} %tokens_hbm.1) | copy-start | bytes 1179652
  5.6 1.0 %copy-start.4 = (f32[256,384]{1,0:T(8,128)S(1)}, f32[256,384]{1,0:T(8,128)}, u32[]{:S(2)}) copy-start(f32[256,384]{1,0:T(8,128)} %noise_w_hbm.1) | copy-start | bytes 1179652
  6.6 0.9 %copy-start.5 = (f32[128,384]{1,0:T(8,128)S(1)}, f32[128,384]{1,0:T(8,128)}, u32[]{:S(2)}) copy-start(f32[128,384]{1,0:T(8,128)} %cond_hbm.1) | copy-start | bytes 589828
  7.6 0.7 copy-start.6
  8.2 0.7 copy-start.7
  8.9 0.7 copy-start.8
  9.6 0.7 copy-start.9
  10.3 0.7 copy-start.10

commit v2 on v1

--- a/solution.py
+++ b/solution.py
@@ -13,8 +13,9 @@
 TOK = 128
 N_ROW = 16
 N_COL = 16
-SLICES = 8
-SLICE_ROWS = TOK // SLICES
+Z = 8
+PIECES = 2
+PIECE_ROWS = TOK // 2 // PIECES
 MSG_ROWS = 56
 MESH = pl.DeviceIdType.MESH
 F32 = jnp.float32
@@ -102,10 +103,10 @@
     parts_in,
     attended,
     load_sems,
-    block_send,
+    source_send,
+    onward_send,
+    mate_send,
     block_recv,
-    mate_send,
-    mate_recv,
     part_send,
     part_recv,
     att_send,
@@ -114,10 +115,16 @@
     row = lax.axis_index("row")
     col = lax.axis_index("col")
     seed = lax.axis_index("seed")
-    core = lax.rem(row, 2)
-    col_y, col_x = col // 2, lax.rem(col, 2)
+    z, core = row // 2, lax.rem(row, 2)
     mate = (row + 1 - 2 * core, col, seed)
-    is_source = core == col_x
+    is_source = row == col
+    far = lax.rem(z + Z - col // 2, Z)
+    is_relay = (far == 2) | (far == 6)
+    onward = jnp.where(far == 2, 1, -1)
+    is_long = is_relay & ((far == 2) == (core == 0))
+
+    def along(delta, which):
+        return (2 * lax.rem(z + Z + delta, Z) + which, col, seed)
 
     pairs = (
         (cond_hbm, cond),
@@ -152,23 +159,25 @@
         )
         return 0
 
-    def greet_source(step, _):
-        source_col = 2 * (2 * step + core) + lax.rem(col, 2)
-
-        @pl.when(jnp.logical_not((row == col) & (source_col == col)))
-        def _():
-            pl.semaphore_signal(
-                barrier, inc=1, device_id=(col, source_col, seed), device_id_type=MESH
-            )
-
-        return 0
-
-    lax.fori_loop(0, SLICES // 2, greet_source, 0)
+    sender_delta = jnp.where(
+        far == 3, -1, jnp.where(far == 5, 1, jnp.where(core == 0, -2, 2))
+    )
+    is_onward = (far >= 3) & (far <= 5)
+    sender = jnp.where(is_onward, along(sender_delta, core)[0], col)
+
+    @pl.when(far != 0)
+    def _():
+        pl.semaphore_signal(
+            barrier, inc=1, device_id=(sender, col, seed), device_id_type=MESH
+        )
+
+    pl.semaphore_signal(barrier, inc=1, device_id=mate, device_id_type=MESH)
     lax.fori_loop(1, N_COL, greet, 0)
-    pl.semaphore_signal(barrier, inc=1, device_id=mate, device_id_type=MESH)
-    to_self = (row == col) & (lax.rem(col_y, 2) == core)
     expected = (
-        N_COL - 1 + 1 + jnp.where(is_source, SLICES, 0) - jnp.where(to_self, 1, 0)
+        N_COL
+        + jnp.where(is_source, 8, 0)
+        + jnp.where(is_relay, 1, 0)
+        + jnp.where(is_long, 1, 0)
     )
 
     for number in (0, 1, 2, 3):
@@ -198,37 +207,67 @@
     loads[5].wait()
     modulated[...] = (
         sigmoid(ada[:, :D]) * layer_norm(tokens[...]) + ada[:, D:]
-    ).reshape(SLICES, SLICE_ROWS, D)
+    ).reshape(2, PIECES, PIECE_ROWS, D)
 
     pl.semaphore_wait(barrier, expected)
 
-    def block_copy(step, piece):
-        target_row = 2 * lax.rem(row // 2 + step, 8) + lax.rem(col_y, 2)
+    def source_copy(place, half, piece):
         return pltpu.make_async_remote_copy(
-            src_ref=modulated.at[piece],
-            dst_ref=block.at[piece],
-            send_sem=block_send.at[step],
-            recv_sem=block_recv.at[piece],
-            device_id=(target_row, row, seed),
+            src_ref=modulated.at[half, piece],
+            dst_ref=block.at[half, piece],
+            send_sem=source_send.at[place, half, piece],
+            recv_sem=block_recv.at[half, piece],
+            device_id=along((2, -2, 1, -1)[place], half),
             device_id_type=MESH,
         )
 
+    def onward_copy(place, piece):
+        return pltpu.make_async_remote_copy(
+            src_ref=block.at[core, piece],
+            dst_ref=block.at[core, piece],
+            send_sem=onward_send.at[place, piece],
+            recv_sem=block_recv.at[core, piece],
+            device_id=along(onward * (place + 1), core),
+            device_id_type=MESH,
+        )
+
+    def mate_copy(source, half, piece):
+        return pltpu.make_async_remote_copy(
+            src_ref=source.at[half, piece],
+            dst_ref=block.at[half, piece],
+            send_sem=mate_send.at[half, piece],
+            recv_sem=block_recv.at[half, piece],
+            device_id=mate,
+            device_id_type=MESH,
+        )
+
+    def arrived(half, piece):
+        mate_copy(block, half, piece).wait_recv()
+
     @pl.when(is_source)
     def _():
-        def send(step, _):
-            place = 7 - step
-
-            @pl.when(jnp.logical_not((place == 0) & to_self))
+        for places in ((0, 1), (2, 3)):
+            for piece in range(PIECES):
+                for place in places:
+                    for half in range(2):
+                        source_copy(place, half, piece).start()
+            if places[0] == 0:
+                for piece in range(PIECES):
+                    for half in range(2):
+                        mate_copy(modulated, half, piece).start()
+        block[...] = modulated[...]
+
+    @pl.when(is_relay)
+    def _():
+        for piece in range(PIECES):
+            arrived(core, piece)
+            onward_copy(0, piece).start()
+
+            @pl.when(is_long)
             def _():
-                block_copy(place, col_y).start()
-
-            return 0
-
-        lax.fori_loop(0, 8, send, 0)
-
-    @pl.when(is_source & to_self)
-    def _():
-        block[pl.ds(col_y, 1)] = modulated[pl.ds(col_y, 1)]
+                onward_copy(1, piece).start()
+
+            mate_copy(block, core, piece).start()
 
     mod_both = stacked(modulated[...].reshape(TOK, D))
     loads[6].wait()
@@ -308,33 +347,41 @@
 
     lax.fori_loop(0, 2 * D // 256, kv_split, 0)
 
-    def mate_copy(piece):
-        return pltpu.make_async_remote_copy(
-            src_ref=block.at[piece],
-            dst_ref=block.at[piece],
-            send_sem=mate_send.at[piece],
-            recv_sem=mate_recv.at[piece],
-            device_id=mate,
-            device_id_type=MESH,
-        )
-
-    def pass_on(step, _):
-        piece = 2 * step + core
-
-        @pl.when(jnp.logical_not(to_self & (piece == col_y)))
-        def _():
-            block_copy(0, piece).wait_recv()
-
-        mate_copy(piece).start()
-        return 0
-
-    lax.fori_loop(0, SLICES // 2, pass_on, 0)
-
-    def from_mate(step, _):
-        mate_copy(2 * step + 1 - core).wait_recv()
-        return 0
-
-    lax.fori_loop(0, SLICES // 2, from_mate, 0)
+    @pl.when((far != 0) & jnp.logical_not(is_relay))
+    def _():
+        for piece in range(PIECES):
+            arrived(core, piece)
+            mate_copy(block, core, piece).start()
+
+    @pl.when(far != 0)
+    def _():
+        for piece in range(PIECES):
+            arrived(1 - core, piece)
+        for piece in range(PIECES):
+            mate_copy(block, core, piece).wait_send()
+
+    @pl.when((far == 0) & jnp.logical_not(is_source))
+    def _():
+        for piece in range(PIECES):
+            for half in range(2):
+                arrived(half, piece)
+
+    @pl.when(is_relay)
+    def _():
+        for piece in range(PIECES):
+            onward_copy(0, piece).wait_send()
+
+            @pl.when(is_long)
+            def _():
+                onward_copy(1, piece).wait_send()
+
+    @pl.when(is_source)
+    def _():
+        for piece in range(PIECES):
+            for half in range(2):
+                for place in range(4):
+                    source_copy(place, half, piece).wait_send()
+                mate_copy(modulated, half, piece).wait_send()
 
     block_both = stacked(block[...].reshape(TOK, D))
 
@@ -417,6 +464,11 @@
         return 0
 
     lax.fori_loop(1, N_COL, part_arrived, 0)
+    def part_sent(step, _):
+        part_copy(lax.rem(col + step, N_COL)).wait_send()
+        return 0
+
+    lax.fori_loop(1, N_COL, part_sent, 0)
     tops = parts_in[:, HEAD_DIM + 1 : HEAD_DIM + 2, :]
     factors = jnp.exp(tops - jnp.max(tops, axis=0, keepdims=True))
     total = jnp.sum(factors * parts_in[:, HEAD_DIM : HEAD_DIM + 1, :], axis=0)
@@ -458,30 +510,11 @@
 
     lax.fori_loop(0, D // 256, out_step, 0)
 
-    @pl.when(is_source)
-    def _():
-        def sent(step, _):
-            @pl.when(jnp.logical_not((step == 0) & to_self))
-            def _():
-                block_copy(step, col_y).wait_send()
-
-            return 0
-
-        lax.fori_loop(0, 8, sent, 0)
-
-    def mate_sent(step, _):
-        mate_copy(2 * step + core).wait_send()
-        return 0
-
-    lax.fori_loop(0, SLICES // 2, mate_sent, 0)
-
-    def parts_sent(step, _):
-        other = lax.rem(col + step, N_COL)
-        part_copy(other).wait_send()
-        att_copy(other, col).wait_send()
-        return 0
-
-    lax.fori_loop(1, N_COL, parts_sent, 0)
+    def att_sent(step, _):
+        att_copy(lax.rem(col + step, N_COL), col).wait_send()
+        return 0
+
+    lax.fori_loop(1, N_COL, att_sent, 0)
 
 
 def body(
@@ -501,7 +534,7 @@
     chain_id,
     residue_index,
 ):
-    hbm = pl.BlockSpec(memory_space=pl.ANY)
+    hbm = pl.BlockSpec(memory_space=pltpu.HBM)
     vmem = pltpu.VMEM
     dma = pltpu.SemaphoreType.DMA
     return pl.pallas_call(
@@ -526,8 +559,8 @@
             vmem((N_ROW, TOK), jnp.int32),
             vmem((N_ROW, TOK), jnp.int32),
             vmem((TOK, 2 * D), F32),
-            vmem((SLICES, SLICE_ROWS, D), F32),
-            vmem((SLICES, SLICE_ROWS, D), F32),
+            vmem((2, PIECES, PIECE_ROWS, D), F32),
+            vmem((2, PIECES, PIECE_ROWS, D), F32),
             vmem((HEADS, 256, TOK), BF16),
             vmem((HEADS, 256, TOK), BF16),
             vmem((TOK, D), F32),
@@ -543,17 +576,17 @@
             vmem((N_COL, MSG_ROWS, TOK), F32),
             vmem((HEADS, HEAD_DIM, TOK), F32),
             dma((14,)),
-            dma((8,)),
-            dma((SLICES,)),
-            dma((SLICES,)),
-            dma((SLICES,)),
+            dma((4, 2, PIECES)),
+            dma((2, PIECES)),
+            dma((2, PIECES)),
+            dma((2, PIECES)),
             dma((N_COL,)),
             dma((N_COL,)),
             dma((N_COL,)),
             dma((N_COL,)),
         ],
         compiler_params=pltpu.CompilerParams(
-            collective_id=0, has_side_effects=True, vmem_limit_bytes=48 * 1024 * 1024
+            collective_id=0, has_side_effects=True, vmem_limit_bytes=60 * 1024 * 1024
         ),
     )(
         tokens_act,

time: 86.8 us -> 68.7 us (0.79)
  the two profiles are of different devices: /device:TPU:1 before, /device:TPU:66 now
where the time goes in v2:
time: 68.7 us; the launch traced here: 68.5 us
  Pallas kernels  66.1 us (96%)
  local copies, waits for them, and re-layouts  1.77 us (3%)
    pallas_call x1, Pallas kernels, body(): pl.pallas_call(kernel, name='attention_block', out_shape=jax.ShapeDtypeSt...  66.1 us
    unnamed x1, local copies, waits for them, and re-layouts  1.77 us

profile of v2, /device:TPU:66, one launch (start us, length us, event | category | flops | bytes accessed | tf_op | source)
XLA Modules:
  0.0 68.5 jit_solution(3027743407821308543)
XLA Ops:
  0.7 66.1 %attention_block.1 = f32[128,768]{1,0:T(8,128)} custom-call(f32[128,768]{1,0:T(8,128)} %tokens_hbm.1, f32[128,384]{1,0:T(8,128)} %cond_hbm.1, f32[1,1]{1,0:T(1,128)} %bitcast.5.noise_ref, f32[2,128]{1,0:T(2,128)} %bitcast.8, f32[2,128]{1,0:T(2,128)} %bitcast.9, f32[256,384]{1,0:T(8,128)} %noise_w_hbm.1, f32[384,1536]{1,0:T(8,128)} %ada_w_hbm.1, ...), custom_call_target="tpu_custom_call" | custom-call | tf_op jit(solution)/shard_map/attention_block/pallas_call | solution.py:540
  66.8 1.8 %copy.18 = f32[128,768]{1,0:T(8,128)} copy(f32[128,768]{1,0:T(8,128)} %attention_block.1) | data formatting | bytes 786432

commit v3 on v2

--- a/solution.py
+++ b/solution.py
@@ -14,7 +14,9 @@
 N_ROW = 16
 N_COL = 16
 Z = 8
-PIECES = 2
+Y = 8
+YS = (4, 3, 5, 2, 6, 1, 7)
+PIECES = 4
 PIECE_ROWS = TOK // 2 // PIECES
 MSG_ROWS = 56
 MESH = pl.DeviceIdType.MESH
@@ -101,15 +103,19 @@
     scores_bias,
     parts_out,
     parts_in,
+    parts_pair,
     attended,
     load_sems,
     source_send,
     onward_send,
     mate_send,
     block_recv,
+    pair_send,
+    pair_recv,
     part_send,
     part_recv,
     att_send,
+    across_send,
     att_recv,
 ):
     row = lax.axis_index("row")
@@ -117,6 +123,8 @@
     seed = lax.axis_index("seed")
     z, core = row // 2, lax.rem(row, 2)
     mate = (row + 1 - 2 * core, col, seed)
+    col_y, col_x = col // 2, lax.rem(col, 2)
+    partner = (row, 2 * col_y + 1 - col_x, seed)
     is_source = row == col
     far = lax.rem(z + Z - col // 2, Z)
     is_relay = (far == 2) | (far == 6)
@@ -127,12 +135,12 @@
         return (2 * lax.rem(z + Z + delta, Z) + which, col, seed)
 
     pairs = (
-        (cond_hbm, cond),
         (freq_hbm, freq),
         (phase_hbm, phase),
         (noise_w_hbm, noise_w),
+        (cond_hbm, cond),
+        (tokens_hbm, tokens),
         (ada_w_hbm, ada_w),
-        (tokens_hbm, tokens),
         (qg_w_hbm, qg_w),
         (chain_hbm, chain),
         (residue_hbm, residue),
@@ -142,11 +150,12 @@
         (kv_w_hbm, kv_w),
         (out_w_hbm, out_w),
     )
-    loads = {}
-    for number, (source, target) in enumerate(pairs):
-        copy = pltpu.make_async_copy(source, target, load_sems.at[number])
-        copy.start()
-        loads[number] = copy
+    loads = {
+        number: pltpu.make_async_copy(source, target, load_sems.at[number])
+        for number, (source, target) in enumerate(pairs)
+    }
+    for number in range(6):
+        loads[number].start()
 
     barrier = pltpu.get_barrier_semaphore()
 
@@ -154,7 +163,7 @@
         pl.semaphore_signal(
             barrier,
             inc=1,
-            device_id=(row, lax.rem(col + step, N_COL), seed),
+            device_id=(row, lax.rem(col + 2 * step, N_COL), seed),
             device_id_type=MESH,
         )
         return 0
@@ -172,30 +181,33 @@
         )
 
     pl.semaphore_signal(barrier, inc=1, device_id=mate, device_id_type=MESH)
-    lax.fori_loop(1, N_COL, greet, 0)
+    pl.semaphore_signal(barrier, inc=1, device_id=partner, device_id_type=MESH)
+    lax.fori_loop(1, Y, greet, 0)
     expected = (
-        N_COL
+        Y
+        + 1
         + jnp.where(is_source, 8, 0)
         + jnp.where(is_relay, 1, 0)
         + jnp.where(is_long, 1, 0)
     )
 
-    for number in (0, 1, 2, 3):
+    for number in (0, 1):
         loads[number].wait()
     level = jnp.full((2, 128), noise_ref[0, 0], F32)
     noise_scaled = 0.25 * jnp.log(level / 16.0)
     features = jnp.cos(2.0 * jnp.pi * (noise_scaled * freq[...] + phase[...]))
-    average = jnp.sum(features, keepdims=True) / 256.0
-    centred = features - average
-    variance = jnp.sum(centred * centred, keepdims=True) / 256.0
-    features = centred * lax.rsqrt(variance + 1e-05)
-    feature_row = jnp.concatenate([features[0:1], features[1:2]], axis=1)
+    feature_row = layer_norm(jnp.concatenate([features[0:1], features[1:2]], axis=1))
     feature_rows = jnp.broadcast_to(feature_row, (16, 256))
+    loads[2].wait()
     noise_high, noise_low = split(noise_w[...])
     shift = dot_split(stacked(feature_rows), noise_high, noise_low)[0:1]
+    loads[3].wait()
     cond_both = stacked(layer_norm(cond[...] + shift))
-
     loads[4].wait()
+    tokens_norm = layer_norm(tokens[...])
+    loads[5].wait()
+    for number in range(6, len(pairs)):
+        loads[number].start()
 
     def ada_step(step, _):
         columns = pl.ds(pl.multiple_of(step * 256, 256), 256)
@@ -203,11 +215,8 @@
         ada[:, columns] = dot_split(cond_both, high, low)
         return 0
 
-    lax.fori_loop(0, 2 * D // 256, ada_step, 0)
-    loads[5].wait()
-    modulated[...] = (
-        sigmoid(ada[:, :D]) * layer_norm(tokens[...]) + ada[:, D:]
-    ).reshape(2, PIECES, PIECE_ROWS, D)
+    lax.fori_loop(0, 2 * D // 256, ada_step, 0, unroll=True)
+    modulated[...] = (sigmoid(ada[:, :D]) * tokens_norm + ada[:, D:]).reshape(2, PIECES, PIECE_ROWS, D)
 
     pl.semaphore_wait(barrier, expected)
 
@@ -261,12 +270,12 @@
     def _():
         for piece in range(PIECES):
             arrived(core, piece)
-            onward_copy(0, piece).start()
 
             @pl.when(is_long)
             def _():
                 onward_copy(1, piece).start()
 
+            onward_copy(0, piece).start()
             mate_copy(block, core, piece).start()
 
     mod_both = stacked(modulated[...].reshape(TOK, D))
@@ -279,7 +288,7 @@
         q_t[columns, :] = result.T
         return 0
 
-    lax.fori_loop(0, D // 256, query_step, 0)
+    lax.fori_loop(0, D // 256, query_step, 0, unroll=True)
 
     def gate_step(step, _):
         columns = pl.ds(pl.multiple_of(step * 256, 256), 256)
@@ -287,7 +296,7 @@
         gates[:, columns] = sigmoid(dot_split(mod_both, high, low))
         return 0
 
-    lax.fori_loop(0, D // 256, gate_step, 0)
+    lax.fori_loop(0, D // 256, gate_step, 0, unroll=True)
     window_row = lax.broadcasted_iota(jnp.int32, (256, TOK), 0)
 
     def window_of(head):
@@ -335,7 +344,7 @@
         out_gate[:, columns] = sigmoid(dot_split(cond_both, high, low))
         return 0
 
-    lax.fori_loop(0, D // 256, out_gate_step, 0)
+    lax.fori_loop(0, D // 256, out_gate_step, 0, unroll=True)
     loads[12].wait()
 
     def kv_split(step, _):
@@ -392,7 +401,7 @@
         k_low[:, columns] = low
         return 0
 
-    lax.fori_loop(0, D // 256, key_step, 0)
+    lax.fori_loop(0, D // 256, key_step, 0, unroll=True)
 
     def value_step(step, _):
         columns = pl.ds(pl.multiple_of(step * 256, 256), 256)
@@ -400,7 +409,7 @@
         v_t[columns, :] = dot_split(block_both, kv_high[:, source], kv_low[:, source]).T
         return 0
 
-    lax.fori_loop(0, D // 256, value_step, 0)
+    lax.fori_loop(0, D // 256, value_step, 0, unroll=True)
 
     ones_rows = jnp.where(lax.broadcasted_iota(jnp.int32, (16, TOK), 0) == 0, 1.0, 0.0)
     tail_row = lax.broadcasted_iota(jnp.int32, (8, TOK), 0)
@@ -427,77 +436,98 @@
         tail = jnp.where(tail_row == 1, top, sums[HEAD_DIM:MSG_ROWS])
         return sums[:HEAD_DIM], tail
 
-    def part_copy(head):
+    def pair_copy(place):
         return pltpu.make_async_remote_copy(
-            src_ref=parts_out.at[head],
-            dst_ref=parts_in.at[col],
-            send_sem=part_send.at[head],
-            recv_sem=part_recv.at[col],
-            device_id=(row, head, seed),
-            device_id_type=MESH,
-        )
-
-    def head_group(group, _):
-        for member in range(3):
-            head = lax.rem(col + 1 + group * 3 + member, HEADS)
+            src_ref=parts_out.at[2 * place + 1 - col_x],
+            dst_ref=parts_pair.at[place],
+            send_sem=pair_send.at[place],
+            recv_sem=pair_recv.at[place],
+            device_id=partner,
+            device_id_type=MESH,
+        )
+
+    def part_copy(place, source):
+        return pltpu.make_async_remote_copy(
+            src_ref=parts_out.at[2 * place + col_x],
+            dst_ref=parts_in.at[source],
+            send_sem=part_send.at[place],
+            recv_sem=part_recv.at[source],
+            device_id=(row, 2 * place + col_x, seed),
+            device_id_type=MESH,
+        )
+
+    places = [lax.rem(col_y + step, Y) for step in YS] + [col_y]
+    for foreign in (True, False):
+        for place in places:
+            head = 2 * place + (1 - col_x if foreign else col_x)
             sums, tail = one_head(head)
             parts_out[head, :HEAD_DIM] = sums
             parts_out[head, HEAD_DIM:] = tail
-            part_copy(head).start()
-        return 0
-
-    lax.fori_loop(0, 5, head_group, 0)
-    sums, tail = one_head(col)
-    parts_in[col, :HEAD_DIM] = sums
-    parts_in[col, HEAD_DIM:] = tail
-
-    def part_arrived(step, _):
-        other = lax.rem(col + N_COL - step, N_COL)
-        pltpu.make_async_remote_copy(
-            src_ref=parts_out.at[other],
-            dst_ref=parts_in.at[other],
-            send_sem=part_send.at[other],
-            recv_sem=part_recv.at[other],
-            device_id=(row, other, seed),
-            device_id_type=MESH,
-        ).wait_recv()
-        return 0
-
-    lax.fori_loop(1, N_COL, part_arrived, 0)
-    def part_sent(step, _):
-        part_copy(lax.rem(col + step, N_COL)).wait_send()
-        return 0
-
-    lax.fori_loop(1, N_COL, part_sent, 0)
+            if foreign:
+                pair_copy(place).start()
+
+    def merged(place):
+        head = 2 * place + col_x
+        pair_copy(place).wait_recv()
+        mine, theirs = parts_out[head], parts_pair[place]
+        top_mine = mine[HEAD_DIM + 1 : HEAD_DIM + 2]
+        top_theirs = theirs[HEAD_DIM + 1 : HEAD_DIM + 2]
+        top = jnp.maximum(top_mine, top_theirs)
+        both = mine * jnp.exp(top_mine - top) + theirs * jnp.exp(top_theirs - top)
+        tail = jnp.where(tail_row == 1, top, both[HEAD_DIM:])
+        return both[:HEAD_DIM], tail
+
+    for place in places[:-1]:
+        head = 2 * place + col_x
+        sums, tail = merged(place)
+        parts_out[head, :HEAD_DIM] = sums
+        parts_out[head, HEAD_DIM:] = tail
+        part_copy(place, col_y).start()
+    sums, tail = merged(col_y)
+    parts_in[col_y, :HEAD_DIM] = sums
+    parts_in[col_y, HEAD_DIM:] = tail
+    for place in places[-2::-1]:
+        part_copy(place, place).wait_recv()
+    for place in places:
+        pair_copy(place).wait_send()
+    for place in places[:-1]:
+        part_copy(place, col_y).wait_send()
     tops = parts_in[:, HEAD_DIM + 1 : HEAD_DIM + 2, :]
     factors = jnp.exp(tops - jnp.max(tops, axis=0, keepdims=True))
     total = jnp.sum(factors * parts_in[:, HEAD_DIM : HEAD_DIM + 1, :], axis=0)
     weighted = jnp.sum(factors * parts_in[:, :HEAD_DIM, :], axis=0)
     attended[pl.ds(col, 1)] = (weighted / total)[None]
 
-    def att_copy(other, place):
+    def att_copy(place):
         return pltpu.make_async_remote_copy(
-            src_ref=attended.at[place],
-            dst_ref=attended.at[place],
-            send_sem=att_send.at[other],
-            recv_sem=att_recv.at[place],
-            device_id=(row, other, seed),
-            device_id_type=MESH,
-        )
-
-    def att_start(step, _):
-        att_copy(lax.rem(col + step, N_COL), col).start()
-        return 0
-
-    lax.fori_loop(1, N_COL, att_start, 0)
+            src_ref=attended.at[col],
+            dst_ref=attended.at[col],
+            send_sem=att_send.at[place],
+            recv_sem=att_recv.at[col],
+            device_id=(row, 2 * place + col_x, seed),
+            device_id_type=MESH,
+        )
+
+    def across_copy(head):
+        return pltpu.make_async_remote_copy(
+            src_ref=attended.at[head],
+            dst_ref=attended.at[head],
+            send_sem=across_send.at[head // 2],
+            recv_sem=att_recv.at[head],
+            device_id=partner,
+            device_id_type=MESH,
+        )
+
+    for place in places[:-1]:
+        att_copy(place).start()
+    across_copy(col).start()
     loads[13].wait()
-
-    def att_arrived(step, _):
-        other = lax.rem(col + N_COL - step, N_COL)
-        att_copy(other, other).wait_recv()
-        return 0
-
-    lax.fori_loop(1, N_COL, att_arrived, 0)
+    for place in places[-2::-1]:
+        head = 2 * place + col_x
+        across_copy(head).wait_recv()
+        across_copy(head).start()
+    for place in places[::-1]:
+        across_copy(2 * place + 1 - col_x).wait_recv()
     gated_both = stacked(gates[...] * attended[...].reshape(D, TOK).T)
 
     def out_step(step, _):
@@ -508,13 +538,12 @@
         )
         return 0
 
-    lax.fori_loop(0, D // 256, out_step, 0)
-
-    def att_sent(step, _):
-        att_copy(lax.rem(col + step, N_COL), col).wait_send()
-        return 0
-
-    lax.fori_loop(1, N_COL, att_sent, 0)
+    lax.fori_loop(0, D // 256, out_step, 0, unroll=True)
+
+    for place in places[:-1]:
+        att_copy(place).wait_send()
+    for place in places:
+        across_copy(2 * place + col_x).wait_send()
 
 
 def body(
@@ -573,16 +602,20 @@
             vmem((D, 2 * D), BF16),
             vmem((HEADS, TOK, TOK), F32),
             vmem((HEADS, MSG_ROWS, TOK), F32),
-            vmem((N_COL, MSG_ROWS, TOK), F32),
+            vmem((Y, MSG_ROWS, TOK), F32),
+            vmem((Y, MSG_ROWS, TOK), F32),
             vmem((HEADS, HEAD_DIM, TOK), F32),
             dma((14,)),
             dma((4, 2, PIECES)),
             dma((2, PIECES)),
             dma((2, PIECES)),
             dma((2, PIECES)),
-            dma((N_COL,)),
-            dma((N_COL,)),
-            dma((N_COL,)),
+            dma((Y,)),
+            dma((Y,)),
+            dma((Y,)),
+            dma((Y,)),
+            dma((Y,)),
+            dma((Y,)),
             dma((N_COL,)),
         ],
         compiler_params=pltpu.CompilerParams(

time: 68.7 us -> 56.6 us (0.82)
  the two profiles are of different devices: /device:TPU:66 before, /device:TPU:1 now
where the time goes in v3:
time: 56.6 us; the launch traced here: 56.4 us
  Pallas kernels  54 us (95%)
  local copies, waits for them, and re-layouts  1.77 us (3%)
  between operations  0.66 us (1%)
    pallas_call x1, Pallas kernels, body(): pl.pallas_call(kernel, name='attention_block', out_shape=jax.ShapeDtypeSt...  54 us
    unnamed x1, local copies, waits for them, and re-layouts  1.77 us

profile of v3, /device:TPU:1, one launch (start us, length us, event | category | flops | bytes accessed | tf_op | source)
XLA Modules:
  0.0 56.4 jit_solution(3229047215275910339)
XLA Ops:
  0.7 54.0 %attention_block.1 = f32[128,768]{1,0:T(8,128)} custom-call(f32[128,768]{1,0:T(8,128)} %tokens_hbm.1, f32[128,384]{1,0:T(8,128)} %cond_hbm.1, f32[1,1]{1,0:T(1,128)} %bitcast.5.noise_ref, f32[2,128]{1,0:T(2,128)} %bitcast.8, f32[2,128]{1,0:T(2,128)} %bitcast.9, f32[256,384]{1,0:T(8,128)} %noise_w_hbm.1, f32[384,1536]{1,0:T(8,128)} %ada_w_hbm.1, ...), custom_call_target="tpu_custom_call" | custom-call | tf_op jit(solution)/shard_map/attention_block/pallas_call | solution.py:569
  54.7 1.8 %copy.18 = f32[128,768]{1,0:T(8,128)} copy(f32[128,768]{1,0:T(8,128)} %attention_block.1) | data formatting | bytes 786432

commit v4 on v3

--- a/solution.py
+++ b/solution.py
@@ -72,7 +72,7 @@
     table_hbm,
     chain_hbm,
     residue_hbm,
-    out_ref,
+    out_hbm,
     tokens,
     cond,
     freq,
@@ -105,7 +105,9 @@
     parts_in,
     parts_pair,
     attended,
+    result,
     load_sems,
+    store_sems,
     source_send,
     onward_send,
     mate_send,
@@ -130,6 +132,8 @@
     is_relay = (far == 2) | (far == 6)
     onward = jnp.where(far == 2, 1, -1)
     is_long = is_relay & ((far == 2) == (core == 0))
+    long_first = col // 2 == 4
+    first_place = jnp.where(long_first, 1, 0)
 
     def along(delta, which):
         return (2 * lax.rem(z + Z + delta, Z) + which, col, seed)
@@ -271,12 +275,16 @@
         for piece in range(PIECES):
             arrived(core, piece)
 
-            @pl.when(is_long)
+            @pl.when(is_long | jnp.logical_not(long_first))
             def _():
-                onward_copy(1, piece).start()
-
-            onward_copy(0, piece).start()
+                onward_copy(first_place, piece).start()
+
             mate_copy(block, core, piece).start()
+        for piece in range(PIECES):
+
+            @pl.when(is_long | long_first)
+            def _():
+                onward_copy(1 - first_place, piece).start()
 
     mod_both = stacked(modulated[...].reshape(TOK, D))
     loads[6].wait()
@@ -299,19 +307,21 @@
     lax.fori_loop(0, D // 256, gate_step, 0, unroll=True)
     window_row = lax.broadcasted_iota(jnp.int32, (256, TOK), 0)
 
-    def window_of(head):
-        return jnp.minimum(head * HEAD_DIM // 128, D // 128 - 2)
-
-    def query_mask(head, _):
-        start = pl.multiple_of(window_of(head) * 128, 128)
-        place = head * HEAD_DIM - start
-        inside = (window_row >= place) & (window_row < place + HEAD_DIM)
-        high, low = split(jnp.where(inside, q_t[pl.ds(start, 256), :], 0.0))
-        q_high[head] = high
-        q_low[head] = low
+    def window_of(half, two):
+        return pl.multiple_of((3 * half + two // 2) * 128, 128)
+
+    def query_mask(number, _):
+        start = window_of(number // 4, lax.rem(number, 4))
+        window = q_t[pl.ds(start, 256), :]
+        for member in range(2):
+            place = (2 * number + member) * HEAD_DIM - start
+            inside = (window_row >= place) & (window_row < place + HEAD_DIM)
+            high, low = split(jnp.where(inside, window, 0.0))
+            q_high[number, :, member * TOK : (member + 1) * TOK] = high
+            q_low[number, :, member * TOK : (member + 1) * TOK] = low
         return 0
 
-    lax.fori_loop(0, HEADS, query_mask, 0)
+    lax.fori_loop(0, HEADS // 2, query_mask, 0)
 
     for number in (7, 8, 9, 10):
         loads[number].wait()
@@ -347,14 +357,17 @@
     lax.fori_loop(0, D // 256, out_gate_step, 0, unroll=True)
     loads[12].wait()
 
-    def kv_split(step, _):
-        columns = pl.ds(pl.multiple_of(step * 256, 256), 256)
-        high, low = split(kv_w[:, columns])
-        kv_high[:, columns] = high
-        kv_low[:, columns] = low
+    def kv_split(part, _):
+        half, kind = part // 2, lax.rem(part, 2)
+        for tile in range(3):
+            source = pl.multiple_of(kind * D + half * 384 + tile * 128, 128)
+            target = pl.multiple_of(half * D + kind * 384 + tile * 128, 128)
+            high, low = split(kv_w[:, pl.ds(source, 128)])
+            kv_high[:, pl.ds(target, 128)] = high
+            kv_low[:, pl.ds(target, 128)] = low
         return 0
 
-    lax.fori_loop(0, 2 * D // 256, kv_split, 0)
+    lax.fori_loop(0, 4, kv_split, 0)
 
     @pl.when((far != 0) & jnp.logical_not(is_relay))
     def _():
@@ -394,51 +407,65 @@
 
     block_both = stacked(block[...].reshape(TOK, D))
 
-    def key_step(step, _):
-        columns = pl.ds(pl.multiple_of(step * 256, 256), 256)
-        high, low = split(dot_split(block_both, kv_high[:, columns], kv_low[:, columns]))
-        k_high[:, columns] = high
-        k_low[:, columns] = low
-        return 0
-
-    lax.fori_loop(0, D // 256, key_step, 0, unroll=True)
-
-    def value_step(step, _):
-        columns = pl.ds(pl.multiple_of(step * 256, 256), 256)
-        source = pl.ds(pl.multiple_of(D + step * 256, 256), 256)
-        v_t[columns, :] = dot_split(block_both, kv_high[:, source], kv_low[:, source]).T
-        return 0
-
-    lax.fori_loop(0, D // 256, value_step, 0, unroll=True)
+    def keys_values(half):
+        for step in range(3):
+            columns = pl.ds(pl.multiple_of(half * D + step * 256, 128), 256)
+            both = dot_split(block_both, kv_high[:, columns], kv_low[:, columns])
+            for tile in range(2):
+                place = 2 * step + tile
+                part = both[:, tile * 128 : (tile + 1) * 128]
+                target = pl.ds(pl.multiple_of(half * 384 + place % 3 * 128, 128), 128)
+                if place < 3:
+                    high, low = split(part)
+                    k_high[:, target] = high
+                    k_low[:, target] = low
+                else:
+                    v_t[target, :] = part.T
 
     ones_rows = jnp.where(lax.broadcasted_iota(jnp.int32, (16, TOK), 0) == 0, 1.0, 0.0)
     tail_row = lax.broadcasted_iota(jnp.int32, (8, TOK), 0)
 
-    def one_head(head):
-        keys = pl.ds(pl.multiple_of(window_of(head) * 128, 128), 256)
-        keys_high, keys_low = k_high[:, keys], k_low[:, keys]
-        queries = q_high[head]
-        scores = (
-            mul(keys_high, queries)
-            + mul(keys_low, queries)
-            + mul(keys_high, q_low[head])
-            + scores_bias[head]
-        )
-        top = jnp.max(scores, axis=0, keepdims=True)
-        weights_high, weights_low = split(jnp.exp(scores - top))
-        values = v_t[pl.ds(pl.multiple_of(head * HEAD_DIM, 16), HEAD_DIM), :]
-        values_high, values_low = split(jnp.concatenate([values, ones_rows], axis=0))
-        sums = (
-            mul(values_high, weights_high)
-            + mul(values_low, weights_high)
-            + mul(values_high, weights_low)
-        )
-        tail = jnp.where(tail_row == 1, top, sums[HEAD_DIM:MSG_ROWS])
-        return sums[:HEAD_DIM], tail
+    none = jnp.zeros((64, TOK), BF16)
+
+    def two_heads(half, two):
+        number = 4 * half + two
+        keys = pl.ds(window_of(half, two), 256)
+        keys_high = k_high[:, keys]
+        queries_low = mul(keys_high, q_low[number])
+        both = mul(jnp.concatenate([keys_high, k_low[:, keys]], axis=0), q_high[number])
+        products = both[:TOK] + both[TOK:] + queries_low
+        tops, highs, lows, values = [], [], [], []
+        for member in range(2):
+            head = 2 * number + member
+            scores = products[:, member * TOK : (member + 1) * TOK] + scores_bias[head]
+            top = jnp.max(scores, axis=0, keepdims=True)
+            high, low = split(jnp.exp(scores - top))
+            tops.append(top)
+            highs.append(high)
+            lows.append(low)
+            value = v_t[pl.ds(pl.multiple_of(head * HEAD_DIM, 16), HEAD_DIM), :]
+            high, low = split(jnp.concatenate([value, ones_rows], axis=0))
+            values.append(jnp.concatenate([high, high], axis=1))
+            values.append(jnp.concatenate([low, none], axis=1))
+        weights = jnp.concatenate(
+            [jnp.concatenate(highs, axis=1), jnp.concatenate(lows, axis=1)], axis=0
+        )
+        sums = mul(jnp.concatenate(values, axis=0), weights)
+        for member in range(2):
+            head = 2 * number + member
+            columns = slice(member * TOK, (member + 1) * TOK)
+            result = (
+                sums[128 * member : 128 * member + 64, columns]
+                + sums[128 * member + 64 : 128 * member + 128, columns]
+            )
+            parts_out[head, :HEAD_DIM] = result[:HEAD_DIM]
+            parts_out[head, HEAD_DIM:] = jnp.where(
+                tail_row == 1, tops[member], result[HEAD_DIM:MSG_ROWS]
+            )
 
     def pair_copy(place):
         return pltpu.make_async_remote_copy(
-            src_ref=parts_out.at[2 * place + 1 - col_x],
+            src_ref=parts_out.at[8 * (1 - col_x) + place],
             dst_ref=parts_pair.at[place],
             send_sem=pair_send.at[place],
             recv_sem=pair_recv.at[place],
@@ -448,7 +475,7 @@
 
     def part_copy(place, source):
         return pltpu.make_async_remote_copy(
-            src_ref=parts_out.at[2 * place + col_x],
+            src_ref=parts_out.at[8 * col_x + place],
             dst_ref=parts_in.at[source],
             send_sem=part_send.at[place],
             recv_sem=part_recv.at[source],
@@ -457,17 +484,18 @@
         )
 
     places = [lax.rem(col_y + step, Y) for step in YS] + [col_y]
-    for foreign in (True, False):
-        for place in places:
-            head = 2 * place + (1 - col_x if foreign else col_x)
-            sums, tail = one_head(head)
-            parts_out[head, :HEAD_DIM] = sums
-            parts_out[head, HEAD_DIM:] = tail
-            if foreign:
-                pair_copy(place).start()
+    twos = [lax.rem(col_y // 2 + step, 4) for step in (2, 1, 3, 0)]
+    keys_values(1 - col_x)
+    for two in twos:
+        two_heads(1 - col_x, two)
+        for member in range(2):
+            pair_copy(2 * two + member).start()
+    keys_values(col_x)
+    for two in twos:
+        two_heads(col_x, two)
 
     def merged(place):
-        head = 2 * place + col_x
+        head = 8 * col_x + place
         pair_copy(place).wait_recv()
         mine, theirs = parts_out[head], parts_pair[place]
         top_mine = mine[HEAD_DIM + 1 : HEAD_DIM + 2]
@@ -478,7 +506,7 @@
         return both[:HEAD_DIM], tail
 
     for place in places[:-1]:
-        head = 2 * place + col_x
+        head = 8 * col_x + place
         sums, tail = merged(place)
         parts_out[head, :HEAD_DIM] = sums
         parts_out[head, HEAD_DIM:] = tail
@@ -496,14 +524,15 @@
     factors = jnp.exp(tops - jnp.max(tops, axis=0, keepdims=True))
     total = jnp.sum(factors * parts_in[:, HEAD_DIM : HEAD_DIM + 1, :], axis=0)
     weighted = jnp.sum(factors * parts_in[:, :HEAD_DIM, :], axis=0)
-    attended[pl.ds(col, 1)] = (weighted / total)[None]
+    own = 8 * col_x + col_y
+    attended[pl.ds(own, 1)] = (weighted / total)[None]
 
     def att_copy(place):
         return pltpu.make_async_remote_copy(
-            src_ref=attended.at[col],
-            dst_ref=attended.at[col],
+            src_ref=attended.at[own],
+            dst_ref=attended.at[own],
             send_sem=att_send.at[place],
-            recv_sem=att_recv.at[col],
+            recv_sem=att_recv.at[own],
             device_id=(row, 2 * place + col_x, seed),
             device_id_type=MESH,
         )
@@ -512,7 +541,7 @@
         return pltpu.make_async_remote_copy(
             src_ref=attended.at[head],
             dst_ref=attended.at[head],
-            send_sem=across_send.at[head // 2],
+            send_sem=across_send.at[lax.rem(head, 8)],
             recv_sem=att_recv.at[head],
             device_id=partner,
             device_id_type=MESH,
@@ -520,30 +549,45 @@
 
     for place in places[:-1]:
         att_copy(place).start()
-    across_copy(col).start()
+    across_copy(own).start()
     loads[13].wait()
     for place in places[-2::-1]:
-        head = 2 * place + col_x
+        head = 8 * col_x + place
         across_copy(head).wait_recv()
         across_copy(head).start()
+
+    def projected(half):
+        rows = pl.ds(pl.multiple_of(half * 384, 128), 384)
+        results = attended[pl.ds(8 * half, 8)].reshape(384, TOK).T
+        gated_both = stacked(gates[:, rows] * results)
+        terms = []
+        for step in range(D // 256):
+            high, low = split(out_w[rows, step * 256 : (step + 1) * 256])
+            terms.append(dot_split(gated_both, high, low))
+        return terms
+
+    for step, term in enumerate(projected(col_x)):
+        ada[:, step * 256 : (step + 1) * 256] = term
     for place in places[::-1]:
-        across_copy(2 * place + 1 - col_x).wait_recv()
-    gated_both = stacked(gates[...] * attended[...].reshape(D, TOK).T)
-
-    def out_step(step, _):
-        columns = pl.ds(pl.multiple_of(step * 256, 256), 256)
-        high, low = split(out_w[:, columns])
-        out_ref[:, columns] = tokens[:, columns] + out_gate[:, columns] * dot_split(
-            gated_both, high, low
-        )
-        return 0
-
-    lax.fori_loop(0, D // 256, out_step, 0, unroll=True)
+        across_copy(8 * (1 - col_x) + place).wait_recv()
+    stores = []
+    for step, term in enumerate(projected(1 - col_x)):
+        columns = slice(step * 256, (step + 1) * 256)
+        result[:, columns] = tokens[:, columns] + out_gate[:, columns] * (
+            term + ada[:, columns]
+        )
+        store = pltpu.make_async_copy(
+            result.at[:, columns], out_hbm.at[:, columns], store_sems.at[step]
+        )
+        store.start()
+        stores.append(store)
 
     for place in places[:-1]:
         att_copy(place).wait_send()
     for place in places:
-        across_copy(2 * place + col_x).wait_send()
+        across_copy(8 * col_x + place).wait_send()
+    for store in stores:
+        store.wait()
 
 
 def body(
@@ -571,7 +615,7 @@
         name="attention_block",
         out_shape=jax.ShapeDtypeStruct((TOK, D), F32),
         in_specs=[hbm, hbm, pl.BlockSpec(memory_space=pltpu.SMEM)] + [hbm] * 12,
-        out_specs=pl.BlockSpec(memory_space=pltpu.VMEM),
+        out_specs=hbm,
         scratch_shapes=[
             vmem((TOK, D), F32),
             vmem((TOK, C_S), F32),
@@ -590,8 +634,8 @@
             vmem((TOK, 2 * D), F32),
             vmem((2, PIECES, PIECE_ROWS, D), F32),
             vmem((2, PIECES, PIECE_ROWS, D), F32),
-            vmem((HEADS, 256, TOK), BF16),
-            vmem((HEADS, 256, TOK), BF16),
+            vmem((HEADS // 2, 256, 2 * TOK), BF16),
+            vmem((HEADS // 2, 256, 2 * TOK), BF16),
             vmem((TOK, D), F32),
             vmem((TOK, D), F32),
             vmem((D, TOK), F32),
@@ -605,7 +649,9 @@
             vmem((Y, MSG_ROWS, TOK), F32),
             vmem((Y, MSG_ROWS, TOK), F32),
             vmem((HEADS, HEAD_DIM, TOK), F32),
+            vmem((TOK, D), F32),
             dma((14,)),
+            dma((3,)),
             dma((4, 2, PIECES)),
             dma((2, PIECES)),
             dma((2, PIECES)),

time: 56.6 us -> 53.6 us (0.947)
  the two profiles are of different devices: /device:TPU:1 before, /device:TPU:8 now
where the time goes in v4:
time: 53.6 us; the launch traced here: 53.5 us
  Pallas kernels  51 us (95%)
  local copies, waits for them, and re-layouts  1.77 us (3%)
  between operations  0.66 us (1%)
    pallas_call x1, Pallas kernels, body(): pl.pallas_call(kernel, name='attention_block', out_shape=jax.ShapeDtypeSt...  51 us
    unnamed x1, local copies, waits for them, and re-layouts  1.77 us

profile of v4, /device:TPU:8, one launch (start us, length us, event | category | flops | bytes accessed | tf_op | source)
XLA Modules:
  0.0 53.5 jit_solution(16523666025940742636)
XLA Ops:
  0.7 51.0 %attention_block.1 = f32[128,768]{1,0:T(8,128)} custom-call(f32[128,768]{1,0:T(8,128)} %tokens_hbm.1, f32[128,384]{1,0:T(8,128)} %cond_hbm.1, f32[1,1]{1,0:T(1,128)} %bitcast.5.noise_ref, f32[2,128]{1,0:T(2,128)} %bitcast.8, f32[2,128]{1,0:T(2,128)} %bitcast.9, f32[256,384]{1,0:T(8,128)} %noise_w_hbm.1, f32[384,1536]{1,0:T(8,128)} %ada_w_hbm.1, ...), custom_call_target="tpu_custom_call" | custom-call | tf_op jit(solution)/shard_map/attention_block/pallas_call | solution.py:613
  51.7 1.8 %copy.18 = f32[128,768]{1,0:T(8,128)} copy(f32[128,768]{1,0:T(8,128)} %attention_block.1) | data formatting | bytes 786432

commit v5 on v4

--- a/solution.py
+++ b/solution.py
@@ -547,9 +547,9 @@
             device_id_type=MESH,
         )
 
-    for place in places[:-1]:
+    across_copy(own).start()
+    for place in places[-2::-1]:
         att_copy(place).start()
-    across_copy(own).start()
     loads[13].wait()
     for place in places[-2::-1]:
         head = 8 * col_x + place

time: 53.6 us -> 53 us (0.989)
  the two profiles are of different devices: /device:TPU:8 before, /device:TPU:66 now
where the time goes in v5:
time: 53 us; the launch traced here: 52.8 us
  Pallas kernels  50.4 us (95%)
  local copies, waits for them, and re-layouts  1.77 us (3%)
  between operations  0.66 us (1%)
    pallas_call x1, Pallas kernels, body(): pl.pallas_call(kernel, name='attention_block', out_shape=jax.ShapeDtypeSt...  50.4 us
    unnamed x1, local copies, waits for them, and re-layouts  1.77 us

profile of v5, /device:TPU:66, one launch (start us, length us, event | category | flops | bytes accessed | tf_op | source)
XLA Modules:
  0.0 52.8 jit_solution(2108825663965711794)
XLA Ops:
  0.7 50.4 %attention_block.1 = f32[128,768]{1,0:T(8,128)} custom-call(f32[128,768]{1,0:T(8,128)} %tokens_hbm.1, f32[128,384]{1,0:T(8,128)} %cond_hbm.1, f32[1,1]{1,0:T(1,128)} %bitcast.5.noise_ref, f32[2,128]{1,0:T(2,128)} %bitcast.8, f32[2,128]{1,0:T(2,128)} %bitcast.9, f32[256,384]{1,0:T(8,128)} %noise_w_hbm.1, f32[384,1536]{1,0:T(8,128)} %ada_w_hbm.1, ...), custom_call_target="tpu_custom_call" | custom-call | tf_op jit(solution)/shard_map/attention_block/pallas_call | solution.py:613
  51.0 1.8 %copy.18 = f32[128,768]{1,0:T(8,128)} copy(f32[128,768]{1,0:T(8,128)} %attention_block.1) | data formatting | bytes 786432
